TPU v7x, 32 devices: a whole 2x2x4 slice. The times are simulated.
32 devices in a mesh: groups: 2 (over x), tensor: 16 (over z, y, core).
Axes of the slice: x: 2, y: 2, z: 4, core: 2. Of those that a mesh axis runs over, the one named last changes fastest.
Arguments:
- queries: bfloat16 [512, 128, 128], P('groups', 'tensor'), parts along dimension 0, may hold values from -4.5 to 4.5
- node_keys: bfloat16 [8, 512, 128], P(None, ('groups', 'tensor')), parts along dimension 1, may hold values from -4.5 to 4.5
- node_values: bfloat16 [8, 512, 128], P(None, ('groups', 'tensor')), parts along dimension 1, may hold values from -15 to 15
- cache_keys: bfloat16 [8, 8192, 128], P(None, ('groups', 'tensor')), parts along dimension 1, may hold values from -4.5 to 4.5
- cache_values: bfloat16 [8, 8192, 128], P(None, ('groups', 'tensor')), parts along dimension 1, may hold values from -15 to 15
- parents: int32 [512], P('groups'), parts along dimension 0, may hold values from -1 to 254, as said below
- out_weight: bfloat16 [16384, 16384], P('tensor'), may hold values from -3 to 3
- residual: bfloat16 [512, 16384], P(('groups', 'tensor')), parts along dimension 0, may hold values from -6 to 6
- norm_gain: bfloat16 [16384], replicated, may hold values from 0.25 to 1.75
Outputs:
- quant_values: bfloat16 [512, 16384], P('groups'), parts along dimension 0
- quant_scales: bfloat16 [512, 128], P('groups'), parts along dimension 0
There are 2 independent parts, one for each index of `groups`. A program takes and returns all parts, laid end to end along the dimension named above; an argument that names none is the same for every part. Nothing has to cross between parts.
Inputs may be any that keep to these rules, and one draw needn't show every extreme that they name: parents[0] is -1 and every other node's parent lies among the 8 nodes before it; the last node's parent is the node before it.
All inputs are finite; a program needn't handle non-finite values. Where the computation divides by a largest or mean magnitude, that divisor is 1e-20 or more.
Results may differ from a plain program's by a relative error of at most 0.015.
Values may be sent and summed in bfloat16 or wider, within the bound.
A program may use at most 192 MiB of HBM per device.

v0:
```python
import math

import jax
import jax.numpy as jnp
from jax import lax
from jax.sharding import PartitionSpec as P

BLK = 128


def hadamard(size):
    rows = jnp.arange(size, dtype=jnp.int32)
    parity = jnp.zeros((size, size), jnp.int32)
    bit = 1
    while bit < size:
        left = (jnp.bitwise_and(rows, bit) > 0).astype(jnp.int32)
        parity = parity + left[:, None] * left[None, :]
        bit = bit * 2
    signs = 1 - 2 * jnp.remainder(parity, 2)
    return signs.astype(jnp.float32) / math.sqrt(size)


def rotate(values, table):
    shape = values.shape
    flat = values.reshape(-1, table.shape[0])
    return jnp.dot(flat, table, precision=lax.Precision.HIGHEST).reshape(shape)


def quantize(values, block):
    count, width = values.shape
    grouped = values.reshape(count, width // block, block)
    scales = (jnp.max(jnp.abs(grouped), axis=-1) + 1e-06).astype(jnp.bfloat16)
    levels = (grouped / scales.astype(jnp.float32)[..., None]).astype(jnp.bfloat16)
    return (levels.reshape(count, width), scales)


def ancestors(parents):
    count = parents.shape[0]
    index = jnp.arange(count, dtype=jnp.int32)
    reach = ((index[None, :] == index[:, None]) | (index[None, :] == parents[:, None])).astype(
        jnp.float32
    )
    for step in range(max(1, (count - 1).bit_length())):
        reach = jnp.minimum(jnp.dot(reach, reach, precision=lax.Precision.HIGHEST), 1.0)
    return reach > 0.5


def shards(
    queries,
    node_keys,
    node_values,
    cache_keys,
    cache_values,
    parents,
    out_weight,
    residual,
    norm_gain,
):
    tok_count, group, head_size = queries.shape
    devices = lax.axis_size("tensor")
    copies = devices // cache_keys.shape[0]
    prefix_keys = jnp.repeat(cache_keys, copies, 0)
    prefix_values = jnp.repeat(cache_values, copies, 0)
    branch_keys = jnp.repeat(node_keys, copies, 0)
    branch_values = jnp.repeat(node_values, copies, 0)
    past_keys, past_values, tree_keys, tree_values = (
        lax.all_to_all(prefix_keys, "tensor", split_axis=0, concat_axis=1, tiled=True),
        lax.all_to_all(prefix_values, "tensor", split_axis=0, concat_axis=1, tiled=True),
        lax.all_to_all(branch_keys, "tensor", split_axis=0, concat_axis=1, tiled=True),
        lax.all_to_all(branch_values, "tensor", split_axis=0, concat_axis=1, tiled=True),
    )
    cache_length = past_keys.shape[1]
    visible = ancestors(parents)
    allowed = jnp.concatenate([jnp.ones((tok_count, cache_length), bool), visible], 1)[:, None, :]
    keys = jnp.concatenate([past_keys[0], tree_keys[0]], 0)
    values = jnp.concatenate([past_values[0], tree_values[0]], 0)
    scores = jnp.einsum(
        "thd,kd->thk", queries, keys, preferred_element_type=jnp.float32
    ) / math.sqrt(head_size)
    scores = jnp.where(allowed, scores, -1e30)
    top = jnp.max(scores, -1, keepdims=True)
    exp_scores = jnp.where(allowed, jnp.exp(scores - top), 0.0)
    totals = jnp.sum(exp_scores, -1, keepdims=True)
    weights = exp_scores.astype(jnp.bfloat16)
    mixed = jnp.einsum("thk,kd->thd", weights, values, preferred_element_type=jnp.float32) / totals
    attended = mixed.astype(jnp.bfloat16).reshape(tok_count, group * head_size)
    table = hadamard(BLK)
    gain = norm_gain.astype(jnp.float32)
    summed = lax.psum_scatter(
        jnp.dot(attended, out_weight, preferred_element_type=jnp.float32).astype(jnp.bfloat16),
        "tensor",
        scatter_dimension=0,
        tiled=True,
    ).astype(jnp.float32)
    state = residual.astype(jnp.float32) + summed
    normed = state * lax.rsqrt(jnp.mean(state * state, -1, keepdims=True) + 1e-05) * gain
    quant_out, scale_out = quantize(rotate(normed, table), BLK)
    quant_values, quant_scales = (
        lax.all_gather(quant_out, "tensor", axis=0, tiled=True),
        lax.all_gather(scale_out, "tensor", axis=0, tiled=True),
    )
    return (quant_values, quant_scales)


def solution(mesh):
    in_specs = (
        P("groups", "tensor", None),
        P(None, ("groups", "tensor"), None),
        P(None, ("groups", "tensor"), None),
        P(None, ("groups", "tensor"), None),
        P(None, ("groups", "tensor"), None),
        P("groups"),
        P("tensor", None),
        P(("groups", "tensor"), None),
        P(),
    )
    out_specs = (P("groups", None), P("groups", None))
    return jax.shard_map(shards, mesh=mesh, in_specs=in_specs, out_specs=out_specs, check_vma=False)
```

profile of v0, /device:TPU:0, one launch (start us, length us, event | category | flops | bytes accessed | tf_op | source)
XLA Modules:
  0.0 374.5 jit_solution(15825816382736828721)
XLA Ops:
  7.2 0.0 copy-start
  7.2 0.8 broadcast_in_dim.28
  8.0 14.1 %all_to_all.16 = bf16[16,16,128]{2,1,0:T(8,128)(2,1)S(1)} all-to-all(bf16[16,16,128]{2,1,0:T(8,128)(2,1)S(1)} %bitcast.68), channel_id=1, replica_groups=mesh['groups'=2,'tensor'=16] {'tensor'}, dimensions={0} | all-to-all | bytes 131072 | tf_op jit(solution)/shard_map/all_to_all | solution.py:69
  22.1 1.4 broadcast_in_dim.32
  23.5 3.5 all-to-all-start.3
  27.0 1.2 copy.24
  28.3 5.6 %all-to-all-done.3 = bf16[16,16,128]{2,1,0:T(8,128)(2,1)S(1)} async-done(((bf16[16,16,128]{2,1,0:T(8,128)(2,1)}), bf16[16,16,128]{2,1,0:T(8,128)(2,1)S(1)}, u32[]{:S(2)}, u32[]{:S(2)}) %all-to-all-start.3) | async-done | bytes 65568 | tf_op jit(solution)/shard_map/all_to_all | solution.py:70
  33.9 0.1 broadcast_in_dim.31
  34.0 27.4 %all_to_all.17 = bf16[16,256,128]{1,2,0:T(8,128)(2,1)S(1)} all-to-all(bf16[16,256,128]{1,2,0:T(8,128)(2,1)S(1)} %bitcast.61), channel_id=1, replica_groups=mesh['groups'=2,'tensor'=16] {'tensor'}, dimensions={0} | all-to-all | bytes 2097152 | tf_op jit(solution)/shard_map/all_to_all | solution.py:68
  61.4 2.2 broadcast_in_dim.27
  63.6 4.9 %all-to-all-start = ((bf16[16,256,128]{2,1,0:T(8,128)(2,1)}), bf16[16,256,128]{2,1,0:T(8,128)(2,1)S(1)}, u32[]{:S(2)}, u32[]{:S(2)}) async-start(bf16[16,256,128]{2,1,0:T(8,128)(2,1)} %bitcast.59), calls=%async_computation | async-start | bytes 2097152 | tf_op jit(solution)/shard_map/all_to_all | solution.py:67
  68.5 0.0 reduce-scatter.2.cloned.1.call-start
  68.6 1.0 convolution_minimum_fusion.7
  69.6 0.4 convolution_minimum_fusion.6
  70.0 0.4 convolution_minimum_fusion.5
  70.4 0.4 convolution_minimum_fusion.4
  70.8 0.4 convolution_minimum_fusion.3
  71.2 0.4 convolution_minimum_fusion.2
  71.6 0.4 convolution_minimum_fusion.1
  71.9 0.4 fusion.13
  72.3 0.2 copy.30
  72.5 1.3 concatenate.9.clone
  73.8 0.1 copy.26
  73.9 1.1 copy.31
  75.0 16.4 %all-to-all-done = bf16[16,256,128]{2,1,0:T(8,128)(2,1)S(1)} async-done(((bf16[16,256,128]{2,1,0:T(8,128)(2,1)}), bf16[16,256,128]{2,1,0:T(8,128)(2,1)S(1)}, u32[]{:S(2)}, u32[]{:S(2)}) %all-to-all-start) | async-done | bytes 1048608 | tf_op jit(solution)/shard_map/all_to_all | solution.py:67
  91.5 0.0 copy-done
  91.5 16.6 %fusion.16 = f32[4352,256,8]{1,0,2:T(8,128)} fusion(bf16[256,128]{1,0:T(8,128)(2,1)S(1)} %bitcast.66, bf16[4096,128]{1,0:T(8,128)(2,1)S(1)} %bitcast.57, bf16[256,8,128]{2,1,0:T(8,128)(2,1)S(1)} %copy-done), kind=kOutput, calls=%fused_computation.25 | convolution fusion | flops 2283929600 | bytes 37289984 | tf_op jit(solution)/shard_map/thd,kd->thk/dot_general | solution.py:77
  108.0 0.0 copy-start.3
  108.0 32.8 %fusion.61 = (f32[256,8]{0,1:T(8,128)S(1)}, bf16[256,8,4352]{0,2,1:T(8,128)(2,1)}) fusion(f32[4352,256,8]{1,0,2:T(8,128)} %fusion.16, pred[256,4352]{0,1:T(8,128)(4,1)} %concatenate.9.clone), kind=kOutput, calls=%fused_computation.88 | output fusion | flops 71307520 | bytes 54599680 | tf_op jit(solution)/shard_map/sub | solution.py:82
  140.8 0.0 copy-done.3
  140.8 8.5 %fusion.10 = bf16[256,8,128]{0,2,1:T(8,128)(2,1)S(1)} fusion(bf16[256,8,4352]{0,2,1:T(8,128)(2,1)} %get-tuple-element.5, bf16[256,128]{0,1:T(8,128)(2,1)S(1)} %copy.26, bf16[4096,128]{0,1:T(8,128)(2,1)S(1)} %bitcast.64, f32[256,8]{0,1:T(8,128)S(1)} %get-tuple-element.4), kind=kOutput, calls=%fused_computation.11 | convolution fusion | flops 2284453888 | bytes 19472384 | tf_op jit(solution)/shard_map/thk,kd->thd/dot_general | solution.py:85
  149.4 0.0 copy-start.4
  149.4 0.0 copy-start.2
  149.4 22.5 %convolution_convert_fusion = bf16[256,16384]{1,0:T(8,128)(2,1)} fusion(bf16[256,1024]{0,1:T(8,128)(2,1)S(1)} %bitcast.65, bf16[1024,16384]{1,0:T(8,128)(2,1)} %param.15), kind=kOutput, calls=%fused_computation.4 | convolution fusion | flops 8594128896 | bytes 42467328 | tf_op jit(solution)/shard_map/dot_general | solution.py:90
  171.9 0.0 copy-start.1
  171.9 0.0 reduce-scatter.2.cloned.1.call-update
  171.9 0.0 all-gather.2.cloned.1.call-start
  172.0 0.0 copy-done.4
  172.0 106.8 %reduce-scatter.2.cloned.1.call-done = bf16[16,16384]{1,0:T(8,128)(2,1)} async-done(((bf16[256,16384]{1,0:T(8,128)(2,1)}), bf16[16,16384]{1,0:T(8,128)(2,1)}) %reduce-scatter.2.cloned.1.call-update) | async-done | bytes 524304 | tf_op jit(solution)/shard_map/reduce_scatter | solution.py:89
  278.8 0.0 copy-done.2
  278.8 1.3 multiply_reduce_fusion
  280.2 1.2 multiply_bitcast_fusion
  281.4 0.2 copy.32
  281.6 1.2 abs_reduce_fusion
  282.8 0.1 divide_convert_fusion
  282.9 0.3 copy.28
  283.2 1.1 copy.37
  284.4 0.0 all-gather.2.cloned.1.call-update
  284.4 20.7 %all_gather.7 = bf16[256,128]{1,0:T(8,128)(2,1)S(1)} all-gather(bf16[16,128]{1,0:T(8,128)(2,1)S(1)} %get-tuple-element.3), channel_id=1, replica_groups=mesh['groups'=2,'tensor'=16] {'tensor'}, dimensions={0}, use_global_device_ids=true | all-gather | bytes 69632 | tf_op jit(solution)/shard_map/all_gather | solution.py:100
  305.1 54.3 %all-gather.2.cloned.1.call-done = bf16[256,16384]{1,0:T(8,128)(2,1)} async-done(((bf16[16,16384]{1,0:T(8,128)(2,1)}), bf16[256,16384]{1,0:T(8,128)(2,1)}) %all-gather.2.cloned.1.call-update) | async-done | bytes 8388624 | tf_op jit(solution)/shard_map/all_gather | solution.py:99
  359.3 7.7 %copy.40 = bf16[256,16384]{1,0:T(8,128)(2,1)} copy(bf16[256,16384]{1,0:T(8,128)(2,1)} %all-gather.2.cloned.1.call-done) | data formatting | bytes 16777216
  367.0 0.6 copy.41
  367.6 0.0 copy-done.1
  (7 shorter events, 0.0 us)
Async XLA Ops:
  7.2 84.3 %copy-start = (bf16[256,8,128]{2,1,0:T(8,128)(2,1)S(1)}, bf16[256,8,128]{2,1,0:T(8,128)(2,1)}, u32[]{:S(2)}) copy-start(bf16[256,8,128]{2,1,0:T(8,128)(2,1)} %param.9) | copy-start | bytes 1572868
  23.5 10.4 %all-to-all-start.3 = ((bf16[16,16,128]{2,1,0:T(8,128)(2,1)}), bf16[16,16,128]{2,1,0:T(8,128)(2,1)S(1)}, u32[]{:S(2)}, u32[]{:S(2)}) async-start(bf16[16,16,128]{2,1,0:T(8,128)(2,1)} %bitcast.7), calls=%async_computation.3 | async-start | bytes 131072 | tf_op jit(solution)/shard_map/all_to_all | solution.py:70
  63.6 27.9 %all-to-all-start = ((bf16[16,256,128]{2,1,0:T(8,128)(2,1)}), bf16[16,256,128]{2,1,0:T(8,128)(2,1)S(1)}, u32[]{:S(2)}, u32[]{:S(2)}) async-start(bf16[16,256,128]{2,1,0:T(8,128)(2,1)} %bitcast.59), calls=%async_computation | async-start | bytes 2097152 | tf_op jit(solution)/shard_map/all_to_all | solution.py:67
  68.5 210.3 %reduce-scatter.2.cloned.1.call-start = ((), (), s32[]{:S(2)}) async-start(), calls=%async_computation.5 | async-start | bytes 8912896 | tf_op jit(solution)/shard_map/reduce_scatter | solution.py:89
  108.0 32.8 %copy-start.3 = (bf16[16,16,8,256]{3,2,0,1:T(8,128)(2,1)S(1)}, bf16[16,16,8,256]{3,2,0,1:T(8,128)(2,1)}, u32[]{:S(2)}) copy-start(bf16[16,16,8,256]{3,2,0,1:T(8,128)(2,1)} %copy.31) | copy-start | bytes 3145732
  149.4 22.6 %copy-start.4 = (bf16[16384]{0:T(1024)(128)(2,1)S(1)}, bf16[16384]{0:T(1024)(128)(2,1)}, u32[]{:S(2)}) copy-start(bf16[16384]{0:T(1024)(128)(2,1)} %param.17) | copy-start | bytes 98308
  149.4 129.4 %copy-start.2 = (bf16[16,16384]{1,0:T(8,128)(2,1)S(1)}, bf16[16,16384]{1,0:T(8,128)(2,1)}, u32[]{:S(2)}) copy-start(bf16[16,16384]{1,0:T(8,128)(2,1)} %param.16) | copy-start | bytes 1572868
  171.9 195.7 %copy-start.1 = (bf16[256,8,128]{2,1,0:T(8,128)(2,1)S(1)}, bf16[256,8,128]{2,1,0:T(8,128)(2,1)}, u32[]{:S(2)}) copy-start(bf16[256,8,128]{2,1,0:T(8,128)(2,1)} %param.9) | copy-start | bytes 1572868
  171.9 187.4 %all-gather.2.cloned.1.call-start = ((), (), s32[]{:S(2)}) async-start(), calls=%async_computation.6 | async-start | bytes 8912896 | tf_op jit(solution)/shard_map/all_gather | solution.py:99
Sparse Core Ops, SparseCore 0:
  172.0 106.7 reduce-scatter.1
  284.5 74.7 all-gather.1
where the time goes:
time: 375 us; the launch traced here: 374 us
  waiting for transfers between devices  183 us (49%)
  blocking collectives  62.2 us (17%)
  matrix products  52.4 us (14%)
  other arithmetic  35.5 us (9%)
  local copies, waits for them, and re-layouts  18.4 us (5%)
  between operations  14.3 us (4%)
  starting transfers between devices  8.5 us (2%)
    reduce_scatter x1, waiting for transfers between devices, shards(): lax.psum_scatter(jnp.dot(attended, out_weight, preferred_element_type=jnp...  107 us
    all_gather x1, waiting for transfers between devices, shards(): lax.all_gather(quant_out, 'tensor', axis=0, tiled=True)  54.3 us
    sub x1, other arithmetic, shards(): exp_scores = jnp.where(allowed, jnp.exp(scores - top), 0.0)  32.8 us
    all_to_all x1, blocking collectives, shards(): lax.all_to_all(prefix_values, 'tensor', split_axis=0, concat_axis=1, tile...  27.4 us
    dot_general x1, matrix products, shards(): jnp.dot(attended, out_weight, preferred_element_type=jnp.float32)  22.5 us
    all_gather x1, blocking collectives, shards(): lax.all_gather(scale_out, 'tensor', axis=0, tiled=True)  20.7 us
    dot_general x1, matrix products, shards(): jnp.einsum('thd,kd->thk', queries, keys, preferred_element_type=jnp.float32)  16.6 us
    all_to_all x1, waiting for transfers between devices, shards(): lax.all_to_all(prefix_keys, 'tensor', split_axis=0, concat_axis=1, tiled=...  16.4 us
  transfers between devices with their start and end apart: 4, of which 4 were waited for; matrix products, arithmetic and copies ran while one was open for 2% of the time, Pallas kernels for 0%

commit v1 on v0

--- a/solution.py
+++ b/solution.py
@@ -1,37 +1,379 @@
+import functools
 import math
 
 import jax
 import jax.numpy as jnp
+import ml_dtypes
+import numpy as np
 from jax import lax
+from jax.experimental import pallas as pl
+from jax.experimental.pallas import tpu as pltpu
 from jax.sharding import PartitionSpec as P
 
 BLK = 128
-
-
-def hadamard(size):
-    rows = jnp.arange(size, dtype=jnp.int32)
-    parity = jnp.zeros((size, size), jnp.int32)
-    bit = 1
-    while bit < size:
-        left = (jnp.bitwise_and(rows, bit) > 0).astype(jnp.int32)
-        parity = parity + left[:, None] * left[None, :]
-        bit = bit * 2
-    signs = 1 - 2 * jnp.remainder(parity, 2)
-    return signs.astype(jnp.float32) / math.sqrt(size)
-
-
-def rotate(values, table):
-    shape = values.shape
-    flat = values.reshape(-1, table.shape[0])
-    return jnp.dot(flat, table, precision=lax.Precision.HIGHEST).reshape(shape)
-
-
-def quantize(values, block):
-    count, width = values.shape
-    grouped = values.reshape(count, width // block, block)
-    scales = (jnp.max(jnp.abs(grouped), axis=-1) + 1e-06).astype(jnp.bfloat16)
-    levels = (grouped / scales.astype(jnp.float32)[..., None]).astype(jnp.bfloat16)
-    return (levels.reshape(count, width), scales)
+MESH = pl.DeviceIdType.MESH
+
+
+def signs(size):
+    index = np.arange(size)
+    both = index[:, None] & index[None, :]
+    parity = np.zeros((size, size), np.int64)
+    while both.any():
+        parity ^= both & 1
+        both = both >> 1
+    return (1 - 2 * parity).astype(ml_dtypes.bfloat16)
+
+
+def ring_chip(pos, chips):
+    turn = chips // 2
+    back = pos // turn
+    return (1 - back) * (2 * pos) + back * (2 * (chips - 1 - pos) + 1)
+
+
+def ring_pos(chip, chips):
+    odd = chip % 2
+    level = chip // 2
+    return (1 - odd) * level + odd * (chips - 1 - level)
+
+
+def send(src, dst, send_sem, recv_sem, target):
+    return pltpu.make_async_remote_copy(
+        src_ref=src,
+        dst_ref=dst,
+        send_sem=send_sem,
+        recv_sem=recv_sem,
+        device_id={"tensor": target},
+        device_id_type=MESH,
+    )
+
+
+def greet(targets):
+    barrier = pltpu.get_barrier_semaphore()
+    for target in targets:
+        pl.semaphore_signal(barrier, inc=1, device_id={"tensor": target}, device_id_type=MESH)
+    pl.semaphore_wait(barrier, len(targets))
+
+
+def project_kernel(
+    devices,
+    att_ref,
+    weight_ref,
+    residual_ref,
+    gain_ref,
+    table_ref,
+    out_ref,
+    wbuf,
+    pair_out,
+    pair_in,
+    part,
+    ring_out,
+    ring_in,
+    swap_out,
+    swap_in,
+    mine,
+    state,
+    packed,
+    w_sem,
+    pair_send,
+    pair_recv,
+    ring_send,
+    ring_recv,
+    swap_send,
+    swap_recv,
+    keep_sem,
+    far_send,
+    far_recv,
+    near_send,
+    near_recv,
+):
+    chips = devices // 2
+    own, width = state.shape
+    rows = 2 * own
+    half_width = width // 2
+    lane = half_width // 4
+    tile = wbuf.shape[2]
+    per = half_width // (2 * tile)
+    total = 4 * per
+    me = lax.axis_index("tensor")
+    core = me % 2
+    chip = me // 2
+    pos = ring_pos(chip, chips)
+    right = 2 * ring_chip((pos + 1) % chips, chips) + core
+    left = 2 * ring_chip((pos + chips - 1) % chips, chips) + core
+    pair = 2 * chip + 1 - core
+
+    def fetch(step):
+        phase = step // per
+        side = (core + 1 + phase % 2) % 2
+        column = side * half_width + ((phase // 2) * per + step % per) * tile
+        return pltpu.make_async_copy(
+            weight_ref.at[:, pl.ds(pl.multiple_of(column, tile), tile)],
+            wbuf.at[step % 3],
+            w_sem.at[step % 3],
+        )
+
+    fetch(0).start()
+    fetch(1).start()
+    greet((pair, left, right))
+
+    def product(step):
+        fetch(step).wait()
+
+        @pl.when(step + 2 < total)
+        def _():
+            fetch(step + 2).start()
+
+        return jnp.dot(att_ref[...], wbuf[step % 3], preferred_element_type=jnp.float32)
+
+    def pair_copy(index):
+        return send(
+            pair_out.at[index], pair_in.at[index], pair_send.at[index], pair_recv.at[index], pair
+        )
+
+    def give(half):
+        def body(i, carry):
+            index = half * per + i
+            pair_out[index] = product(2 * half * per + i).astype(jnp.bfloat16)
+            pair_copy(index).start()
+            return carry
+
+        lax.fori_loop(0, per, body, 0)
+
+    def keep(half):
+        def body(i, carry):
+            index = half * per + i
+            own_part = product((2 * half + 1) * per + i)
+            pair_copy(index).wait_recv()
+            part[:, pl.ds(pl.multiple_of(index * tile, tile), tile)] = own_part + pair_in[
+                index
+            ].astype(jnp.float32)
+            return carry
+
+        lax.fori_loop(0, per, body, 0)
+
+    def ring_copy(stream, step):
+        return send(
+            ring_out.at[stream, step],
+            ring_in.at[stream, step],
+            ring_send.at[stream, step],
+            ring_recv.at[stream, step],
+            left if stream % 2 else right,
+        )
+
+    def ring_step(stream, step, first):
+        if stream % 2:
+            target = (pos + 1 + step) % chips
+        else:
+            target = (pos + chips - 1 - step) % chips
+        row = pl.multiple_of(ring_chip(target, chips) * rows, rows)
+        value = part[pl.ds(row, rows), stream * lane : (stream + 1) * lane]
+        if not first:
+            ring_copy(stream, step - 1).wait_recv()
+            value = value + ring_in[stream, step - 1].astype(jnp.float32)
+        ring_out[stream, step] = value.astype(jnp.bfloat16)
+        ring_copy(stream, step).start()
+
+    give(0)
+    keep(0)
+    ring_step(0, 0, True)
+    ring_step(1, 0, True)
+    give(1)
+    ring_step(0, 1, False)
+    ring_step(1, 1, False)
+    keep(1)
+    ring_step(2, 0, True)
+    ring_step(3, 0, True)
+
+    def around(step, carry):
+        for stream in (0, 1):
+            ring_step(stream, step, False)
+        for stream in (2, 3):
+            ring_step(stream, step - 1, False)
+        return carry
+
+    lax.fori_loop(2, chips - 1, around, 0)
+    for stream in (2, 3):
+        ring_step(stream, chips - 2, False)
+    row = pl.multiple_of(chip * rows, rows)
+    for stream in range(4):
+        ring_copy(stream, chips - 2).wait_recv()
+        columns = slice(stream * lane, (stream + 1) * lane)
+        mine[:, columns] = part[pl.ds(row, rows), columns] + ring_in[stream, chips - 2].astype(
+            jnp.float32
+        )
+    swap_out[...] = mine[pl.ds(pl.multiple_of((1 - core) * own, own), own), :]
+    swap = send(swap_out, swap_in, swap_send, swap_recv, pair)
+    swap.start()
+    state[:, pl.ds(pl.multiple_of(core * half_width, half_width), half_width)] = mine[
+        pl.ds(pl.multiple_of(core * own, own), own), :
+    ]
+    swap.wait_recv()
+    state[:, pl.ds(pl.multiple_of((1 - core) * half_width, half_width), half_width)] = swap_in[...]
+
+    group = 8
+    step_width = group * BLK
+
+    def squares(i, acc):
+        columns = pl.ds(pl.multiple_of(i * step_width, step_width), step_width)
+        value = state[:, columns] + residual_ref[:, columns].astype(jnp.float32)
+        state[:, columns] = value
+        return acc + value * value
+
+    acc = lax.fori_loop(
+        0, width // step_width, squares, jnp.zeros((own, step_width), jnp.float32)
+    )
+    inverse = lax.rsqrt(jnp.sum(acc, axis=1, keepdims=True) / width + 1e-05)
+    table = table_ref[...]
+    lanes = lax.broadcasted_iota(jnp.int32, (own, width // BLK), 1)
+
+    def rotate_group(i, scales):
+        blocks = []
+        for b in range(group):
+            columns = pl.ds(pl.multiple_of(i * step_width + b * BLK, BLK), BLK)
+            blocks.append(
+                state[:, columns] * inverse * gain_ref[:, columns].astype(jnp.float32)
+            )
+        normed = jnp.concatenate(blocks, axis=0)
+        high = normed.astype(jnp.bfloat16)
+        low = (normed - high.astype(jnp.float32)).astype(jnp.bfloat16)
+        rotated = (
+            jnp.dot(high, table, preferred_element_type=jnp.float32)
+            + jnp.dot(low, table, preferred_element_type=jnp.float32)
+        ) * (1.0 / math.sqrt(BLK))
+        scale = (
+            (jnp.max(jnp.abs(rotated), axis=1, keepdims=True) + 1e-06)
+            .astype(jnp.bfloat16)
+            .astype(jnp.float32)
+        )
+        levels = (rotated / scale).astype(jnp.bfloat16)
+        for b in range(group):
+            columns = pl.ds(pl.multiple_of(i * step_width + b * BLK, BLK), BLK)
+            packed[:, columns] = levels[b * own : (b + 1) * own, :]
+            scales = jnp.where(lanes == i * group + b, scale[b * own : (b + 1) * own, :], scales)
+        return scales
+
+    scales = lax.fori_loop(
+        0, width // step_width, rotate_group, jnp.zeros((own, width // BLK), jnp.float32)
+    )
+    packed[:, width:] = scales.astype(jnp.bfloat16)
+
+    full = packed.shape[1]
+    cut = (full // 2 // BLK) * BLK
+    pieces = (pl.ds(0, cut), pl.ds(cut, full - cut))
+    hops = chips // 2
+
+    def owner(d, hop):
+        where = (pos + hop) % chips if d else (pos + chips - hop) % chips
+        return 2 * ring_chip(where, chips) + core
+
+    def far_copy(d, hop, piece):
+        block = owner(d, hop - 1)
+        dst = out_ref.at[block, :, pieces[piece]]
+        src = packed.at[:, pieces[piece]] if hop == 1 else dst
+        at = (d * hops + hop - 1) * 2 + piece
+        return send(src, dst, far_send.at[at], far_recv.at[at], left if d else right)
+
+    def near_copy(d, hop, piece):
+        block = owner(d, hop)
+        dst = out_ref.at[block, :, pieces[piece]]
+        src = packed.at[:, pieces[piece]] if hop == 0 else dst
+        at = (d * (hops + 1) + hop) * 2 + piece
+        return send(src, dst, near_send.at[at], near_recv.at[at], pair)
+
+    def goes(d, hop, piece):
+        return hop < hops or piece == d
+
+    order = ((0, 0), (1, 1), (0, 1), (1, 0))
+    for d, piece in order:
+        far_copy(d, 1, piece).start()
+    own_copy = pltpu.make_async_copy(packed, out_ref.at[me], keep_sem)
+    own_copy.start()
+    for piece in (0, 1):
+        near_copy(0, 0, piece).start()
+    for hop in range(1, hops + 1):
+        for d, piece in order:
+            if goes(d, hop, piece):
+                far_copy(d, hop, piece).wait_recv()
+                if hop < hops and goes(d, hop + 1, piece):
+                    far_copy(d, hop + 1, piece).start()
+                near_copy(d, hop, piece).start()
+    own_copy.wait()
+    for piece in (0, 1):
+        near_copy(0, 0, piece).wait()
+    for hop in range(1, hops + 1):
+        for d, piece in order:
+            if goes(d, hop, piece):
+                far_copy(d, hop, piece).wait_send()
+                near_copy(d, hop, piece).wait()
+    swap.wait_send()
+
+    def drain_pair(i, carry):
+        pair_copy(i).wait_send()
+        return carry
+
+    lax.fori_loop(0, 2 * per, drain_pair, 0)
+
+    def drain_ring(step, carry):
+        for stream in range(4):
+            ring_copy(stream, step).wait_send()
+        return carry
+
+    lax.fori_loop(0, chips - 1, drain_ring, 0)
+
+
+def project(devices, attended, out_weight, residual, norm_gain):
+    tok_count, depth = attended.shape
+    width = out_weight.shape[1]
+    own = residual.shape[0]
+    chips = devices // 2
+    hops = chips // 2
+    half_width = width // 2
+    lane = half_width // 4
+    tile = half_width // 8
+    full = width + width // BLK
+    bf16, f32 = jnp.bfloat16, jnp.float32
+    dma = pltpu.SemaphoreType.DMA
+    vmem = pl.BlockSpec(memory_space=pltpu.VMEM)
+    hbm = pl.BlockSpec(memory_space=pl.ANY)
+    return pl.pallas_call(
+        functools.partial(project_kernel, devices),
+        out_shape=jax.ShapeDtypeStruct((devices, own, full), bf16),
+        in_specs=[vmem, hbm, vmem, vmem, vmem],
+        out_specs=hbm,
+        scratch_shapes=[
+            pltpu.VMEM((3, depth, tile), bf16),
+            pltpu.VMEM((8, tok_count, tile), bf16),
+            pltpu.VMEM((8, tok_count, tile), bf16),
+            pltpu.VMEM((tok_count, half_width), f32),
+            pltpu.VMEM((4, chips - 1, 2 * own, lane), bf16),
+            pltpu.VMEM((4, chips - 1, 2 * own, lane), bf16),
+            pltpu.VMEM((own, half_width), f32),
+            pltpu.VMEM((own, half_width), f32),
+            pltpu.VMEM((2 * own, half_width), f32),
+            pltpu.VMEM((own, width), f32),
+            pltpu.VMEM((own, full), bf16),
+            dma((3,)),
+            dma((8,)),
+            dma((8,)),
+            dma((4, chips - 1)),
+            dma((4, chips - 1)),
+            dma,
+            dma,
+            dma,
+            dma((4 * hops,)),
+            dma((4 * hops,)),
+            dma((4 * (hops + 1),)),
+            dma((4 * (hops + 1),)),
+        ],
+        compiler_params=pltpu.CompilerParams(
+            collective_id=0, has_side_effects=True, vmem_limit_bytes=52 * 1024 * 1024
+        ),
+        cost_estimate=pl.CostEstimate(
+            flops=2 * tok_count * depth * width,
+            bytes_accessed=2 * depth * width,
+            transcendentals=0,
+        ),
+    )(attended, out_weight, residual, norm_gain.reshape(1, -1), jnp.asarray(signs(BLK)))
 
 
 def ancestors(parents):
@@ -84,22 +426,12 @@
     weights = exp_scores.astype(jnp.bfloat16)
     mixed = jnp.einsum("thk,kd->thd", weights, values, preferred_element_type=jnp.float32) / totals
     attended = mixed.astype(jnp.bfloat16).reshape(tok_count, group * head_size)
-    table = hadamard(BLK)
-    gain = norm_gain.astype(jnp.float32)
-    summed = lax.psum_scatter(
-        jnp.dot(attended, out_weight, preferred_element_type=jnp.float32).astype(jnp.bfloat16),
-        "tensor",
-        scatter_dimension=0,
-        tiled=True,
-    ).astype(jnp.float32)
-    state = residual.astype(jnp.float32) + summed
-    normed = state * lax.rsqrt(jnp.mean(state * state, -1, keepdims=True) + 1e-05) * gain
-    quant_out, scale_out = quantize(rotate(normed, table), BLK)
-    quant_values, quant_scales = (
-        lax.all_gather(quant_out, "tensor", axis=0, tiled=True),
-        lax.all_gather(scale_out, "tensor", axis=0, tiled=True),
-    )
-    return (quant_values, quant_scales)
+    gathered = project(devices, attended, out_weight, residual, norm_gain)
+    width = out_weight.shape[1]
+    return (
+        gathered[:, :, :width].reshape(tok_count, width),
+        gathered[:, :, width:].reshape(tok_count, width // BLK),
+    )
 
 
 def solution(mesh):

time: 375 us -> 260 us (0.69)
  waiting for transfers between devices: 183 us -> 21.3 us
  Pallas kernels: 0 us -> 107 us
  matrix products: 52.4 us -> 28.8 us
  blocking collectives: 62.2 us -> 41.5 us
  between operations: 14.3 us -> 0.81 us
    pallas_call x0 -> x1, Pallas kernels: none -> 107 us  [project(): pl.pallas_call(functools.partial(project_kernel, devices), out_shape=jax....]
    reduce_scatter x1 -> x0, waiting for transfers between devices: 107 us -> none  [shards(): lax.psum_scatter(jnp.dot(attended, out_weight, preferred_element_type=jnp...]
    all_gather x1 -> x0, waiting for transfers between devices: 54.3 us -> none  [shards(): lax.all_gather(quant_out, 'tensor', axis=0, tiled=True)]
    dot_general x2 -> x0, matrix products: 23.6 us -> none  [the longest x1 22.5 us: shards(): jnp.dot(attended, out_weight, preferred_element_type=jnp.float32)]
    all_gather x1 -> x0, blocking collectives: 20.7 us -> none  [shards(): lax.all_gather(scale_out, 'tensor', axis=0, tiled=True)]
    unnamed x16 -> x12, local copies, waits for them, and re-layouts: 11.1 us -> 1.45 us
    slice x0 -> x2, local copies, waits for them, and re-layouts: none -> 9.13 us  [the longest x1 7.66 us: shards(): gathered[:, :, :width].reshape(tok_count, width)]
  transfers between devices with their start and end apart: 4 -> 2, of which waited for: 4 -> 2; matrix products, arithmetic and copies ran while one was open for 2% -> 3% of each run, Pallas kernels for 0% -> 0%
where the time goes in v1:
time: 260 us; the launch traced here: 259 us
  Pallas kernels  107 us (41%)
  blocking collectives  41.5 us (16%)
  other arithmetic  32.8 us (13%)
  matrix products  28.8 us (11%)
  waiting for transfers between devices  21.3 us (8%)
  local copies, waits for them, and re-layouts  18.6 us (7%)
  starting transfers between devices  8.42 us (3%)
    pallas_call x1, Pallas kernels, project(): pl.pallas_call(functools.partial(project_kernel, devices), out_shape=jax....  107 us
    sub x1, other arithmetic, shards(): exp_scores = jnp.where(allowed, jnp.exp(scores - top), 0.0)  32.8 us
    all_to_all x1, blocking collectives, shards(): lax.all_to_all(prefix_values, 'tensor', split_axis=0, concat_axis=1, tile...  27.4 us
    dot_general x1, matrix products, shards(): jnp.einsum('thd,kd->thk', queries, keys, preferred_element_type=jnp.float32)  16.6 us
    all_to_all x1, waiting for transfers between devices, shards(): lax.all_to_all(prefix_keys, 'tensor', split_axis=0, concat_axis=1, tiled=...  15.7 us
    all_to_all x1, blocking collectives, shards(): lax.all_to_all(branch_keys, 'tensor', split_axis=0, concat_axis=1, tiled=...  14.1 us
    dot_general x1, matrix products, shards(): jnp.einsum('thk,kd->thd', weights, values, preferred_element_type=jnp.flo...  8.59 us
    slice x1, local copies, waits for them, and re-layouts, shards(): gathered[:, :, :width].reshape(tok_count, width)  7.66 us
  transfers between devices with their start and end apart: 2, of which 2 were waited for; matrix products, arithmetic and copies ran while one was open for 3% of the time, Pallas kernels for 0%

profile of v1, /device:TPU:0, one launch (start us, length us, event | category | flops | bytes accessed | tf_op | source)
XLA Modules:
  0.0 259.4 jit_solution(7419390828516703286)
XLA Ops:
  0.6 0.0 copy-start
  0.6 0.8 broadcast_in_dim.40
  1.5 14.1 %all_to_all.16 = bf16[16,16,128]{2,1,0:T(8,128)(2,1)S(1)} all-to-all(bf16[16,16,128]{2,1,0:T(8,128)(2,1)S(1)} %bitcast.53), channel_id=1, replica_groups=mesh['groups'=2,'tensor'=16] {'tensor'}, dimensions={0} | all-to-all | bytes 131072 | tf_op jit(solution)/shard_map/all_to_all | solution.py:411
  15.6 1.4 broadcast_in_dim.44
  17.0 3.5 %all-to-all-start.3 = ((bf16[16,16,128]{2,1,0:T(8,128)(2,1)}), bf16[16,16,128]{2,1,0:T(8,128)(2,1)S(1)}, u32[]{:S(2)}, u32[]{:S(2)}) async-start(bf16[16,16,128]{2,1,0:T(8,128)(2,1)} %bitcast.7), calls=%async_computation.3 | async-start | bytes 131072 | tf_op jit(solution)/shard_map/all_to_all | solution.py:412
  20.5 1.2 copy.26
  21.7 5.6 %all-to-all-done.3 = bf16[16,16,128]{2,1,0:T(8,128)(2,1)S(1)} async-done(((bf16[16,16,128]{2,1,0:T(8,128)(2,1)}), bf16[16,16,128]{2,1,0:T(8,128)(2,1)S(1)}, u32[]{:S(2)}, u32[]{:S(2)}) %all-to-all-start.3) | async-done | bytes 65568 | tf_op jit(solution)/shard_map/all_to_all | solution.py:412
  27.3 0.1 broadcast_in_dim.43
  27.4 27.4 %all_to_all.17 = bf16[16,256,128]{1,2,0:T(8,128)(2,1)S(1)} all-to-all(bf16[16,256,128]{1,2,0:T(8,128)(2,1)S(1)} %bitcast.48), channel_id=1, replica_groups=mesh['groups'=2,'tensor'=16] {'tensor'}, dimensions={0} | all-to-all | bytes 2097152 | tf_op jit(solution)/shard_map/all_to_all | solution.py:410
  54.9 2.2 broadcast_in_dim.39
  57.1 4.9 %all-to-all-start = ((bf16[16,256,128]{2,1,0:T(8,128)(2,1)}), bf16[16,256,128]{2,1,0:T(8,128)(2,1)S(1)}, u32[]{:S(2)}, u32[]{:S(2)}) async-start(bf16[16,256,128]{2,1,0:T(8,128)(2,1)} %bitcast.47), calls=%async_computation | async-start | bytes 2097152 | tf_op jit(solution)/shard_map/all_to_all | solution.py:409
  62.0 1.0 convolution_minimum_fusion.7
  63.0 0.4 convolution_minimum_fusion.6
  63.4 0.4 convolution_minimum_fusion.5
  63.8 0.4 convolution_minimum_fusion.4
  64.2 0.4 convolution_minimum_fusion.3
  64.6 0.4 convolution_minimum_fusion.2
  65.0 0.4 convolution_minimum_fusion.1
  65.4 0.4 fusion.13
  65.8 0.2 copy.33
  65.9 0.8 reshape.53.gain_ref
  66.7 1.3 concatenate.9.clone
  68.0 0.1 copy.28
  68.1 1.1 copy.34
  69.3 15.7 %all-to-all-done = bf16[16,256,128]{2,1,0:T(8,128)(2,1)S(1)} async-done(((bf16[16,256,128]{2,1,0:T(8,128)(2,1)}), bf16[16,256,128]{2,1,0:T(8,128)(2,1)S(1)}, u32[]{:S(2)}, u32[]{:S(2)}) %all-to-all-start) | async-done | bytes 1048608 | tf_op jit(solution)/shard_map/all_to_all | solution.py:409
  84.9 0.0 copy-done
  84.9 16.6 %fusion.16 = f32[4352,256,8]{1,0,2:T(8,128)} fusion(bf16[256,128]{1,0:T(8,128)(2,1)S(1)} %bitcast.51, bf16[4096,128]{1,0:T(8,128)(2,1)S(1)} %bitcast.45, bf16[256,8,128]{2,1,0:T(8,128)(2,1)S(1)} %copy-done), kind=kOutput, calls=%fused_computation.24 | convolution fusion | flops 2283929600 | bytes 37289984 | tf_op jit(solution)/shard_map/thd,kd->thk/dot_general | solution.py:419
  101.5 0.0 copy-start.4
  101.5 32.8 %fusion.27 = (f32[256,8]{0,1:T(8,128)S(1)}, bf16[256,8,4352]{0,2,1:T(8,128)(2,1)}) fusion(f32[4352,256,8]{1,0,2:T(8,128)} %fusion.16, pred[256,4352]{0,1:T(8,128)(4,1)} %concatenate.9.clone), kind=kOutput, calls=%fused_computation.36 | output fusion | flops 71307520 | bytes 54599680 | tf_op jit(solution)/shard_map/sub | solution.py:424
  134.3 0.0 copy-done.4
  134.3 0.0 copy-start.2
  134.3 0.0 copy-start.3
  134.3 8.6 %fusion.10 = bf16[256,8,128]{0,2,1:T(8,128)(2,1)S(1)} fusion(bf16[256,8,4352]{0,2,1:T(8,128)(2,1)} %get-tuple-element.3, bf16[256,128]{0,1:T(8,128)(2,1)S(1)} %copy.28, bf16[4096,128]{0,1:T(8,128)(2,1)S(1)} %bitcast.49, f32[256,8]{0,1:T(8,128)S(1)} %get-tuple-element.2), kind=kOutput, calls=%fused_computation.10 | convolution fusion | flops 2284453888 | bytes 19472384 | tf_op jit(solution)/shard_map/thk,kd->thd/dot_general | solution.py:427
  142.9 0.2 copy.32.att_ref
  143.1 0.0 copy-done.2
  143.1 0.0 copy-done.3
  143.1 0.0 copy-start.1
  143.1 107.1 %shard_map.113 = bf16[16,16,16512]{2,1,0:T(8,128)(2,1)} custom-call(bf16[256,1024]{1,0:T(8,128)(2,1)S(1)} %copy.32.att_ref, bf16[1024,16384]{1,0:T(8,128)(2,1)} %weight_ref.1, bf16[16,16384]{1,0:T(8,128)(2,1)S(1)} %copy-done.2, bf16[1,16384]{1,0:T(2,128)(2,1)S(1)} %reshape.53.gain_ref, bf16[128,128]{1,0:T(8,128)(2,1)S(1)} %copy-done.3), custom_call_target="tpu_custom_call" | custom-call | flops 8589934592 | bytes 33554432 | tf_op jit(solution)/shard_map/pallas_call | solution.py:338
  250.3 7.7 %slice.6 = bf16[16,16,16384]{2,1,0:T(8,128)(2,1)} slice(bf16[16,16,16512]{2,1,0:T(8,128)(2,1)} %shard_map.113), slice={[0:16], [0:16], [0:16384]} | slice | bytes 16777216 | tf_op jit(solution)/shard_map/slice | solution.py:432
  257.9 1.5 slice.7
  259.4 0.0 copy-done.1
Async XLA Ops:
  0.6 84.3 %copy-start = (bf16[256,8,128]{2,1,0:T(8,128)(2,1)S(1)}, bf16[256,8,128]{2,1,0:T(8,128)(2,1)}, u32[]{:S(2)}) copy-start(bf16[256,8,128]{2,1,0:T(8,128)(2,1)} %param.10) | copy-start | bytes 1572868
  17.0 10.4 %all-to-all-start.3 = ((bf16[16,16,128]{2,1,0:T(8,128)(2,1)}), bf16[16,16,128]{2,1,0:T(8,128)(2,1)S(1)}, u32[]{:S(2)}, u32[]{:S(2)}) async-start(bf16[16,16,128]{2,1,0:T(8,128)(2,1)} %bitcast.7), calls=%async_computation.3 | async-start | bytes 131072 | tf_op jit(solution)/shard_map/all_to_all | solution.py:412
  57.1 27.9 %all-to-all-start = ((bf16[16,256,128]{2,1,0:T(8,128)(2,1)}), bf16[16,256,128]{2,1,0:T(8,128)(2,1)S(1)}, u32[]{:S(2)}, u32[]{:S(2)}) async-start(bf16[16,256,128]{2,1,0:T(8,128)(2,1)} %bitcast.47), calls=%async_computation | async-start | bytes 2097152 | tf_op jit(solution)/shard_map/all_to_all | solution.py:409
  101.5 32.8 %copy-start.4 = (bf16[16,16,8,256]{3,2,0,1:T(8,128)(2,1)S(1)}, bf16[16,16,8,256]{3,2,0,1:T(8,128)(2,1)}, u32[]{:S(2)}) copy-start(bf16[16,16,8,256]{3,2,0,1:T(8,128)(2,1)} %copy.34) | copy-start | bytes 3145732
  134.3 8.8 %copy-start.2 = (bf16[16,16384]{1,0:T(8,128)(2,1)S(1)}, bf16[16,16384]{1,0:T(8,128)(2,1)}, u32[]{:S(2)}) copy-start(bf16[16,16384]{1,0:T(8,128)(2,1)} %residual_ref.1) | copy-start | bytes 1572868
  134.3 8.8 %copy-start.3 = (bf16[128,128]{1,0:T(8,128)(2,1)S(1)}, bf16[128,128]{1,0:T(8,128)(2,1)}, u32[]{:S(2)}) copy-start(bf16[128,128]{1,0:T(8,128)(2,1)} %constant.17.clone.table_ref) | copy-start | bytes 98308
  143.1 116.3 %copy-start.1 = (bf16[256,8,128]{2,1,0:T(8,128)(2,1)S(1)}, bf16[256,8,128]{2,1,0:T(8,128)(2,1)}, u32[]{:S(2)}) copy-start(bf16[256,8,128]{2,1,0:T(8,128)(2,1)} %param.10) | copy-start | bytes 1572868

commit v2 on v1

--- a/solution.py
+++ b/solution.py
@@ -376,15 +376,215 @@
     )(attended, out_weight, residual, norm_gain.reshape(1, -1), jnp.asarray(signs(BLK)))
 
 
-def ancestors(parents):
-    count = parents.shape[0]
-    index = jnp.arange(count, dtype=jnp.int32)
-    reach = ((index[None, :] == index[:, None]) | (index[None, :] == parents[:, None])).astype(
-        jnp.float32
+def attend_kernel(
+    devices,
+    query_ref,
+    node_key_ref,
+    node_value_ref,
+    cache_key_ref,
+    cache_value_ref,
+    parent_ref,
+    out_ref,
+    keys,
+    values,
+    tree_keys,
+    tree_values,
+    acc,
+    top,
+    bias,
+    far_send,
+    far_recv,
+    near_send,
+    near_recv,
+    keep_sem,
+):
+    heads, tok_count, size = query_ref.shape
+    chips = devices // 2
+    spread = chips // cache_key_ref.shape[0]
+    length = cache_key_ref.shape[1]
+    me = lax.axis_index("tensor")
+    core = me % 2
+    chip = me // 2
+    pair = 2 * chip + 1 - core
+    low = pl.ds(0, size)
+    sources = (cache_key_ref, cache_value_ref, node_key_ref, node_value_ref)
+
+    def place(a, offset, block):
+        return (
+            keys.at[offset, core],
+            values.at[offset, core, :, low],
+            tree_keys.at[block],
+            tree_values.at[block, :, low],
+        )[a]
+
+    def far_copy(a, offset):
+        target = (chip + offset) % chips
+        return send(
+            sources[a].at[target // spread],
+            place(a, offset, me),
+            far_send.at[a, offset],
+            far_recv.at[a, offset],
+            2 * target + core,
+        )
+
+    def near_copy(a, offset):
+        block = 2 * ((chip + chips - offset) % chips) + core
+        here = place(a, offset, block)
+        src = sources[a].at[chip // spread] if isinstance(offset, int) and offset == 0 else here
+        return send(src, here, near_send.at[a, offset], near_recv.at[a, offset], pair)
+
+    def keep_copy(a):
+        return pltpu.make_async_copy(
+            sources[a].at[chip // spread], place(a, 0, me), keep_sem.at[a]
+        )
+
+    for a in range(4):
+        keep_copy(a).start()
+    values[:, :, :, size:] = jnp.ones(values.shape[:3] + (size,), jnp.bfloat16)
+    tree_values[:, :, size:] = jnp.ones(tree_values.shape[:2] + (size,), jnp.bfloat16)
+    greet([pair] + [2 * ((chip + o) % chips) + core for o in range(1, chips)])
+
+    def scatter(offset, carry):
+        for a in range(4):
+            far_copy(a, offset).start()
+        return carry
+
+    lax.fori_loop(1, chips, scatter, 0)
+    for a in range(4):
+        near_copy(a, 0).start()
+
+    index = lax.broadcasted_iota(jnp.int32, (tok_count, tok_count), 0)
+    other = lax.broadcasted_iota(jnp.int32, (tok_count, tok_count), 1)
+    reach = jnp.where((other == index) | (other == parent_ref[...]), 1.0, 0.0)
+
+    def extend(step, reach):
+        held = reach.astype(jnp.bfloat16)
+        return jnp.minimum(jnp.dot(held, held, preferred_element_type=jnp.float32), 1.0)
+
+    reach = lax.fori_loop(0, max(1, (tok_count - 1).bit_length()), extend, reach)
+    bias[...] = jnp.where(reach > 0.5, 0.0, -1e30)
+
+    factor = math.log2(math.e) / math.sqrt(size)
+
+    def attend(key, value, first, masked):
+        def body(head, carry):
+            scores = (
+                lax.dot_general(
+                    query_ref[head],
+                    key,
+                    (((1,), (1,)), ((), ())),
+                    preferred_element_type=jnp.float32,
+                )
+                * factor
+            )
+            if masked:
+                scores = scores + bias[...]
+            peak = jnp.max(scores, axis=1, keepdims=True)
+            if not first:
+                before = top[head][:, :1]
+                peak = jnp.maximum(peak, before)
+            weights = jnp.exp2(scores - peak).astype(jnp.bfloat16)
+            mixed = jnp.dot(weights, value, preferred_element_type=jnp.float32)
+            if not first:
+                mixed = mixed + acc[head] * jnp.exp2(before - peak)
+            if masked:
+                columns = pl.ds(pl.multiple_of(head * size, size), size)
+                out_ref[:, columns] = (mixed[:, :size] / mixed[:, size:]).astype(jnp.bfloat16)
+            else:
+                acc[head] = mixed
+                top[head] = jnp.broadcast_to(peak, (tok_count, size))
+            return carry
+
+        lax.fori_loop(0, heads, body, 0, unroll=2)
+
+    def collect(offset):
+        for a in range(4):
+            far_copy(a, offset).wait_recv()
+            near_copy(a, offset).start()
+
+    def chunk(j):
+        for offset in (2 * j, 2 * j + 1):
+            for a in range(4):
+                near_copy(a, offset).wait_recv()
+        span = pl.ds(2 * j, 2)
+        attend(
+            keys[span].reshape(4 * length, size),
+            values[span].reshape(4 * length, 2 * size),
+            isinstance(j, int) and j == 0,
+            False,
+        )
+
+    for a in range(4):
+        keep_copy(a).wait()
+    collect(1)
+    collect(2)
+    collect(3)
+    chunk(0)
+
+    def advance(j, carry):
+        collect(2 * j + 2)
+        collect(2 * j + 3)
+        chunk(j)
+        return carry
+
+    lax.fori_loop(1, chips // 2 - 1, advance, 0)
+    chunk(chips // 2 - 1)
+    attend(
+        tree_keys[...].reshape(tok_count, size),
+        tree_values[...].reshape(tok_count, 2 * size),
+        False,
+        True,
     )
-    for step in range(max(1, (count - 1).bit_length())):
-        reach = jnp.minimum(jnp.dot(reach, reach, precision=lax.Precision.HIGHEST), 1.0)
-    return reach > 0.5
+
+    def drain(offset, carry):
+        for a in range(4):
+            far_copy(a, offset).wait_send()
+            near_copy(a, offset).wait_send()
+        return carry
+
+    for a in range(4):
+        near_copy(a, 0).wait_send()
+    lax.fori_loop(1, chips, drain, 0)
+
+
+def attend(devices, queries, node_keys, node_values, cache_keys, cache_values, parents):
+    heads, tok_count, size = queries.shape
+    chips = devices // 2
+    length = cache_keys.shape[1]
+    nodes = node_keys.shape[1]
+    bf16, f32 = jnp.bfloat16, jnp.float32
+    dma = pltpu.SemaphoreType.DMA
+    vmem = pl.BlockSpec(memory_space=pltpu.VMEM)
+    hbm = pl.BlockSpec(memory_space=pl.ANY)
+    seen = devices * (length + nodes)
+    return pl.pallas_call(
+        functools.partial(attend_kernel, devices),
+        out_shape=jax.ShapeDtypeStruct((tok_count, heads * size), bf16),
+        in_specs=[vmem, hbm, hbm, hbm, hbm, vmem],
+        out_specs=vmem,
+        scratch_shapes=[
+            pltpu.VMEM((chips, 2, length, size), bf16),
+            pltpu.VMEM((chips, 2, length, 2 * size), bf16),
+            pltpu.VMEM((devices, nodes, size), bf16),
+            pltpu.VMEM((devices, nodes, 2 * size), bf16),
+            pltpu.VMEM((heads, tok_count, 2 * size), f32),
+            pltpu.VMEM((heads, tok_count, size), f32),
+            pltpu.VMEM((tok_count, tok_count), f32),
+            dma((4, chips)),
+            dma((4, chips)),
+            dma((4, chips)),
+            dma((4, chips)),
+            dma((4,)),
+        ],
+        compiler_params=pltpu.CompilerParams(
+            collective_id=1, has_side_effects=True, vmem_limit_bytes=48 * 1024 * 1024
+        ),
+        cost_estimate=pl.CostEstimate(
+            flops=4 * tok_count * heads * seen * size,
+            bytes_accessed=4 * seen * size,
+            transcendentals=tok_count * heads * seen,
+        ),
+    )(queries, node_keys, node_values, cache_keys, cache_values, parents.reshape(-1, 1))
 
 
 def shards(
@@ -398,34 +598,17 @@
     residual,
     norm_gain,
 ):
-    tok_count, group, head_size = queries.shape
+    tok_count = queries.shape[0]
     devices = lax.axis_size("tensor")
-    copies = devices // cache_keys.shape[0]
-    prefix_keys = jnp.repeat(cache_keys, copies, 0)
-    prefix_values = jnp.repeat(cache_values, copies, 0)
-    branch_keys = jnp.repeat(node_keys, copies, 0)
-    branch_values = jnp.repeat(node_values, copies, 0)
-    past_keys, past_values, tree_keys, tree_values = (
-        lax.all_to_all(prefix_keys, "tensor", split_axis=0, concat_axis=1, tiled=True),
-        lax.all_to_all(prefix_values, "tensor", split_axis=0, concat_axis=1, tiled=True),
-        lax.all_to_all(branch_keys, "tensor", split_axis=0, concat_axis=1, tiled=True),
-        lax.all_to_all(branch_values, "tensor", split_axis=0, concat_axis=1, tiled=True),
+    attended = attend(
+        devices,
+        jnp.transpose(queries, (1, 0, 2)),
+        node_keys,
+        node_values,
+        cache_keys,
+        cache_values,
+        parents,
     )
-    cache_length = past_keys.shape[1]
-    visible = ancestors(parents)
-    allowed = jnp.concatenate([jnp.ones((tok_count, cache_length), bool), visible], 1)[:, None, :]
-    keys = jnp.concatenate([past_keys[0], tree_keys[0]], 0)
-    values = jnp.concatenate([past_values[0], tree_values[0]], 0)
-    scores = jnp.einsum(
-        "thd,kd->thk", queries, keys, preferred_element_type=jnp.float32
-    ) / math.sqrt(head_size)
-    scores = jnp.where(allowed, scores, -1e30)
-    top = jnp.max(scores, -1, keepdims=True)
-    exp_scores = jnp.where(allowed, jnp.exp(scores - top), 0.0)
-    totals = jnp.sum(exp_scores, -1, keepdims=True)
-    weights = exp_scores.astype(jnp.bfloat16)
-    mixed = jnp.einsum("thk,kd->thd", weights, values, preferred_element_type=jnp.float32) / totals
-    attended = mixed.astype(jnp.bfloat16).reshape(tok_count, group * head_size)
     gathered = project(devices, attended, out_weight, residual, norm_gain)
     width = out_weight.shape[1]
     return (

time: 260 us -> 174 us (0.67)
  Pallas kernels: 107 us -> 158 us
  blocking collectives: 41.5 us -> 0 us
  other arithmetic: 32.8 us -> 0 us
  matrix products: 28.8 us -> 0 us
  waiting for transfers between devices: 21.3 us -> 0 us
  starting transfers between devices: 8.42 us -> 0 us
  local copies, waits for them, and re-layouts: 18.6 us -> 15.5 us
    pallas_call x0 -> x1, Pallas kernels: none -> 47.9 us  [attend(): pl.pallas_call(functools.partial(attend_kernel, devices), out_shape=jax.S...]
    all_to_all x2 -> x0, blocking collectives: 41.5 us -> none  [the longest x1 27.4 us: shards(): lax.all_to_all(prefix_values, 'tensor', split_axis=0, concat_axis=1, tile...]
    sub x1 -> x0, other arithmetic: 32.8 us -> none  [shards(): exp_scores = jnp.where(allowed, jnp.exp(scores - top), 0.0)]
    dot_general x10 -> x0, matrix products: 28.8 us -> none  [the longest x1 16.6 us: shards(): jnp.einsum('thd,kd->thk', queries, keys, preferred_element_type=jnp.float32)]
    all_to_all x2 -> x0, waiting for transfers between devices: 21.3 us -> none  [the longest x1 15.7 us: shards(): lax.all_to_all(prefix_keys, 'tensor', split_axis=0, concat_axis=1, tiled=...]
    all_to_all x2 -> x0, starting transfers between devices: 8.42 us -> none  [the longest x1 4.92 us: shards(): lax.all_to_all(prefix_keys, 'tensor', split_axis=0, concat_axis=1, tiled=...]
    broadcast_in_dim x4 -> x0, local copies, waits for them, and re-layouts: 4.53 us -> none  [the longest x1 2.21 us: shards(): prefix_keys = jnp.repeat(cache_keys, copies, 0)]
    unnamed x12 -> x13, local copies, waits for them, and re-layouts: 1.45 us -> 4.78 us
  transfers between devices with their start and end apart: 2 -> 0, of which waited for: 2 -> 0; matrix products, arithmetic and copies ran while one was open for 3% -> 0% of each run, Pallas kernels for 0% -> 0%
where the time goes in v2:
time: 174 us
  Pallas kernels  158 us (91%)
  local copies, waits for them, and re-layouts  15.5 us (9%)
    pallas_call x1, Pallas kernels, project(): pl.pallas_call(functools.partial(project_kernel, devices), out_shape=jax....  110 us
    pallas_call x1, Pallas kernels, attend(): pl.pallas_call(functools.partial(attend_kernel, devices), out_shape=jax.S...  47.9 us
    slice x1, local copies, waits for them, and re-layouts, shards(): gathered[:, :, :width].reshape(tok_count, width)  7.65 us
    unnamed x13, local copies, waits for them, and re-layouts  4.78 us

profile of v2, /device:TPU:0, one launch (start us, length us, event | category | flops | bytes accessed | tf_op | source)
XLA Modules:
  0.0 173.8 jit_solution(1892045378282975573)
XLA Ops:
  0.6 0.8 reshape.17.gain_ref
  1.4 0.8 copy.14.parent_ref
  2.2 1.1 copy.16
  3.4 0.0 copy-start
  3.4 0.0 copy-start.1
  3.4 0.0 copy-start.2
  3.4 1.1 copy-done.2
  4.5 0.0 copy-start.3
  4.5 1.0 copy-done.3
  5.5 0.0 copy-start.4
  5.5 0.8 copy-done.4
  6.3 0.0 copy-start.5
  6.3 0.8 copy-done.5
  7.0 47.9 %shard_map.113.att_ref = bf16[256,1024]{1,0:T(8,128)(2,1)S(1)} custom-call(bf16[8,256,128]{2,1,0:T(8,128)(2,1)S(1)} %bitcast.6, bf16[8,16,128]{2,1,0:T(8,128)(2,1)S(1)} %copy-done.4, bf16[8,16,128]{2,1,0:T(8,128)(2,1)S(1)} %copy-done.5, bf16[8,256,128]{2,1,0:T(8,128)(2,1)S(1)} %copy-done.2, bf16[8,256,128]{2,1,0:T(8,128)(2,1)S(1)} %copy-done.3, ...), custom_call_target="tpu_custom_call" | custom-call | flops 4563402752 | bytes 2228224 | tf_op jit(solution)/shard_map/pallas_call | solution.py:560
  54.9 0.0 copy-done
  54.9 0.0 copy-done.1
  54.9 109.7 %shard_map.114 = bf16[16,16,16512]{2,1,0:T(8,128)(2,1)} custom-call(bf16[256,1024]{1,0:T(8,128)(2,1)S(1)} %shard_map.113.att_ref, bf16[1024,16384]{1,0:T(8,128)(2,1)} %weight_ref.1, bf16[16,16384]{1,0:T(8,128)(2,1)S(1)} %copy-done, bf16[1,16384]{1,0:T(2,128)(2,1)S(1)} %reshape.17.gain_ref, bf16[128,128]{1,0:T(8,128)(2,1)S(1)} %copy-done.1), custom_call_target="tpu_custom_call" | custom-call | flops 8589934592 | bytes 33554432 | tf_op jit(solution)/shard_map/pallas_call | solution.py:338
  164.7 1.5 slice.7
  166.1 7.7 %slice.6 = bf16[16,16,16384]{2,1,0:T(8,128)(2,1)} slice(bf16[16,16,16512]{2,1,0:T(8,128)(2,1)} %shard_map.114), slice={[0:16], [0:16], [0:16384]} | slice | bytes 16777216 | tf_op jit(solution)/shard_map/slice | solution.py:615
Async XLA Ops:
  3.4 51.6 %copy-start = (bf16[16,16384]{1,0:T(8,128)(2,1)S(1)}, bf16[16,16384]{1,0:T(8,128)(2,1)}, u32[]{:S(2)}) copy-start(bf16[16,16384]{1,0:T(8,128)(2,1)} %residual_ref.1) | copy-start | bytes 1572868
  3.4 51.6 %copy-start.1 = (bf16[128,128]{1,0:T(8,128)(2,1)S(1)}, bf16[128,128]{1,0:T(8,128)(2,1)}, u32[]{:S(2)}) copy-start(bf16[128,128]{1,0:T(8,128)(2,1)} %constant.2.clone.table_ref) | copy-start | bytes 98308
  3.4 1.1 copy-start.2
  4.5 1.0 copy-start.3
  5.5 0.8 copy-start.4
  6.3 0.8 copy-start.5

commit v3 on v2

--- a/solution.py
+++ b/solution.py
@@ -62,6 +62,7 @@
     gain_ref,
     table_ref,
     out_ref,
+    scale_ref,
     wbuf,
     pair_out,
     pair_in,
@@ -73,6 +74,7 @@
     mine,
     state,
     packed,
+    packed_scales,
     w_sem,
     pair_send,
     pair_recv,
@@ -255,11 +257,18 @@
     scales = lax.fori_loop(
         0, width // step_width, rotate_group, jnp.zeros((own, width // BLK), jnp.float32)
     )
-    packed[:, width:] = scales.astype(jnp.bfloat16)
-
-    full = packed.shape[1]
-    cut = (full // 2 // BLK) * BLK
-    pieces = (pl.ds(0, cut), pl.ds(cut, full - cut))
+    packed_scales[...] = scales.astype(jnp.bfloat16)
+
+    cut = width // 2
+
+    def view(block, piece):
+        if piece == 2:
+            return scale_ref.at[block]
+        return out_ref.at[block, :, pl.ds(piece * cut, cut)]
+
+    def fresh(piece):
+        return packed_scales if piece == 2 else packed.at[:, pl.ds(piece * cut, cut)]
+
     hops = chips // 2
 
     def owner(d, hop):
@@ -268,27 +277,31 @@
 
     def far_copy(d, hop, piece):
         block = owner(d, hop - 1)
-        dst = out_ref.at[block, :, pieces[piece]]
-        src = packed.at[:, pieces[piece]] if hop == 1 else dst
-        at = (d * hops + hop - 1) * 2 + piece
+        dst = view(block, piece)
+        src = fresh(piece) if hop == 1 else dst
+        at = (d * hops + hop - 1) * 3 + piece
         return send(src, dst, far_send.at[at], far_recv.at[at], left if d else right)
 
     def near_copy(d, hop, piece):
         block = owner(d, hop)
-        dst = out_ref.at[block, :, pieces[piece]]
-        src = packed.at[:, pieces[piece]] if hop == 0 else dst
-        at = (d * (hops + 1) + hop) * 2 + piece
+        dst = view(block, piece)
+        src = fresh(piece) if hop == 0 else dst
+        at = (d * (hops + 1) + hop) * 3 + piece
         return send(src, dst, near_send.at[at], near_recv.at[at], pair)
 
     def goes(d, hop, piece):
-        return hop < hops or piece == d
-
-    order = ((0, 0), (1, 1), (0, 1), (1, 0))
+        return hop < hops or piece == d or (piece == 2 and d == 0)
+
+    order = ((0, 0), (1, 1), (0, 1), (1, 0), (0, 2), (1, 2))
     for d, piece in order:
         far_copy(d, 1, piece).start()
-    own_copy = pltpu.make_async_copy(packed, out_ref.at[me], keep_sem)
-    own_copy.start()
-    for piece in (0, 1):
+    own_copies = (
+        pltpu.make_async_copy(packed, out_ref.at[me], keep_sem.at[0]),
+        pltpu.make_async_copy(packed_scales, scale_ref.at[me], keep_sem.at[1]),
+    )
+    for own_copy in own_copies:
+        own_copy.start()
+    for piece in range(3):
         near_copy(0, 0, piece).start()
     for hop in range(1, hops + 1):
         for d, piece in order:
@@ -297,8 +310,9 @@
                 if hop < hops and goes(d, hop + 1, piece):
                     far_copy(d, hop + 1, piece).start()
                 near_copy(d, hop, piece).start()
-    own_copy.wait()
-    for piece in (0, 1):
+    for own_copy in own_copies:
+        own_copy.wait()
+    for piece in range(3):
         near_copy(0, 0, piece).wait()
     for hop in range(1, hops + 1):
         for d, piece in order:
@@ -330,16 +344,19 @@
     half_width = width // 2
     lane = half_width // 4
     tile = half_width // 8
-    full = width + width // BLK
+    blocks = width // BLK
     bf16, f32 = jnp.bfloat16, jnp.float32
     dma = pltpu.SemaphoreType.DMA
     vmem = pl.BlockSpec(memory_space=pltpu.VMEM)
     hbm = pl.BlockSpec(memory_space=pl.ANY)
     return pl.pallas_call(
         functools.partial(project_kernel, devices),
-        out_shape=jax.ShapeDtypeStruct((devices, own, full), bf16),
+        out_shape=(
+            jax.ShapeDtypeStruct((devices, own, width), bf16),
+            jax.ShapeDtypeStruct((devices, own, blocks), bf16),
+        ),
         in_specs=[vmem, hbm, vmem, vmem, vmem],
-        out_specs=hbm,
+        out_specs=(hbm, hbm),
         scratch_shapes=[
             pltpu.VMEM((3, depth, tile), bf16),
             pltpu.VMEM((8, tok_count, tile), bf16),
@@ -351,7 +368,8 @@
             pltpu.VMEM((own, half_width), f32),
             pltpu.VMEM((2 * own, half_width), f32),
             pltpu.VMEM((own, width), f32),
-            pltpu.VMEM((own, full), bf16),
+            pltpu.VMEM((own, width), bf16),
+            pltpu.VMEM((own, blocks), bf16),
             dma((3,)),
             dma((8,)),
             dma((8,)),
@@ -359,14 +377,14 @@
             dma((4, chips - 1)),
             dma,
             dma,
-            dma,
-            dma((4 * hops,)),
-            dma((4 * hops,)),
-            dma((4 * (hops + 1),)),
-            dma((4 * (hops + 1),)),
+            dma((2,)),
+            dma((6 * hops,)),
+            dma((6 * hops,)),
+            dma((6 * (hops + 1),)),
+            dma((6 * (hops + 1),)),
         ],
         compiler_params=pltpu.CompilerParams(
-            collective_id=0, has_side_effects=True, vmem_limit_bytes=52 * 1024 * 1024
+            collective_id=0, has_side_effects=True, vmem_limit_bytes=58 * 1024 * 1024
         ),
         cost_estimate=pl.CostEstimate(
             flops=2 * tok_count * depth * width,
@@ -444,12 +462,18 @@
     tree_values[:, :, size:] = jnp.ones(tree_values.shape[:2] + (size,), jnp.bfloat16)
     greet([pair] + [2 * ((chip + o) % chips) + core for o in range(1, chips)])
 
-    def scatter(offset, carry):
-        for a in range(4):
+    def scatter_nodes(offset, carry):
+        for a in (2, 3):
             far_copy(a, offset).start()
         return carry
 
-    lax.fori_loop(1, chips, scatter, 0)
+    def scatter_cache(offset, carry):
+        for a in (0, 1):
+            far_copy(a, offset).start()
+        return carry
+
+    lax.fori_loop(1, chips, scatter_nodes, 0)
+    lax.fori_loop(1, chips, scatter_cache, 0)
     for a in range(4):
         near_copy(a, 0).start()
 
@@ -466,7 +490,7 @@
 
     factor = math.log2(math.e) / math.sqrt(size)
 
-    def attend(key, value, first, masked):
+    def attend(key, value, first, last):
         def body(head, carry):
             scores = (
                 lax.dot_general(
@@ -477,7 +501,7 @@
                 )
                 * factor
             )
-            if masked:
+            if first:
                 scores = scores + bias[...]
             peak = jnp.max(scores, axis=1, keepdims=True)
             if not first:
@@ -487,7 +511,7 @@
             mixed = jnp.dot(weights, value, preferred_element_type=jnp.float32)
             if not first:
                 mixed = mixed + acc[head] * jnp.exp2(before - peak)
-            if masked:
+            if last:
                 columns = pl.ds(pl.multiple_of(head * size, size), size)
                 out_ref[:, columns] = (mixed[:, :size] / mixed[:, size:]).astype(jnp.bfloat16)
             else:
@@ -497,44 +521,58 @@
 
         lax.fori_loop(0, heads, body, 0, unroll=2)
 
-    def collect(offset):
-        for a in range(4):
+    def collect(offset, which):
+        for a in which:
             far_copy(a, offset).wait_recv()
             near_copy(a, offset).start()
 
-    def chunk(j):
+    def settle(offset, which):
+        for a in which:
+            near_copy(a, offset).wait_recv()
+
+    def chunk(j, last):
         for offset in (2 * j, 2 * j + 1):
-            for a in range(4):
-                near_copy(a, offset).wait_recv()
+            settle(offset, (0, 1))
         span = pl.ds(2 * j, 2)
         attend(
             keys[span].reshape(4 * length, size),
             values[span].reshape(4 * length, 2 * size),
-            isinstance(j, int) and j == 0,
             False,
+            last,
         )
 
     for a in range(4):
         keep_copy(a).wait()
-    collect(1)
-    collect(2)
-    collect(3)
-    chunk(0)
-
-    def advance(j, carry):
-        collect(2 * j + 2)
-        collect(2 * j + 3)
-        chunk(j)
-        return carry
-
-    lax.fori_loop(1, chips // 2 - 1, advance, 0)
-    chunk(chips // 2 - 1)
+
+    def collect_nodes(offset, carry):
+        collect(offset, (2, 3))
+        return carry
+
+    def settle_nodes(offset, carry):
+        settle(offset, (2, 3))
+        return carry
+
+    lax.fori_loop(1, chips, collect_nodes, 0)
+    lax.fori_loop(0, chips, settle_nodes, 0)
     attend(
         tree_keys[...].reshape(tok_count, size),
         tree_values[...].reshape(tok_count, 2 * size),
+        True,
         False,
-        True,
     )
+    collect(1, (0, 1))
+    chunk(0, False)
+
+    def advance(j, carry):
+        collect(2 * j, (0, 1))
+        collect(2 * j + 1, (0, 1))
+        chunk(j, False)
+        return carry
+
+    lax.fori_loop(1, chips // 2 - 1, advance, 0)
+    collect(chips - 2, (0, 1))
+    collect(chips - 1, (0, 1))
+    chunk(chips // 2 - 1, True)
 
     def drain(offset, carry):
         for a in range(4):
@@ -577,7 +615,7 @@
             dma((4,)),
         ],
         compiler_params=pltpu.CompilerParams(
-            collective_id=1, has_side_effects=True, vmem_limit_bytes=48 * 1024 * 1024
+            collective_id=1, has_side_effects=True, vmem_limit_bytes=60 * 1024 * 1024
         ),
         cost_estimate=pl.CostEstimate(
             flops=4 * tok_count * heads * seen * size,
@@ -609,12 +647,9 @@
         cache_values,
         parents,
     )
-    gathered = project(devices, attended, out_weight, residual, norm_gain)
+    levels, scales = project(devices, attended, out_weight, residual, norm_gain)
     width = out_weight.shape[1]
-    return (
-        gathered[:, :, :width].reshape(tok_count, width),
-        gathered[:, :, width:].reshape(tok_count, width // BLK),
-    )
+    return (levels.reshape(tok_count, width), scales.reshape(tok_count, width // BLK))
 
 
 def solution(mesh):

time: 174 us -> 171 us (0.983)
  local copies, waits for them, and re-layouts: 15.5 us -> 13.1 us
    slice x2 -> x0, local copies, waits for them, and re-layouts: 9.13 us -> none  [the longest x1 7.65 us: shards(): gathered[:, :, :width].reshape(tok_count, width)]
    unnamed x13 -> x5, local copies, waits for them, and re-layouts: 4.78 us -> 10.2 us
    pallas_call x1, Pallas kernels: 110 us -> 106 us  [project(): pl.pallas_call(functools.partial(project_kernel, devices), out_shape=(jax...]
    pallas_call x1, Pallas kernels: 47.9 us -> 50.4 us  [attend(): pl.pallas_call(functools.partial(attend_kernel, devices), out_shape=jax.S...]
where the time goes in v3:
time: 171 us; the launch traced here: 170 us
  Pallas kernels  157 us (92%)
  local copies, waits for them, and re-layouts  13.1 us (8%)
    pallas_call x1, Pallas kernels, project(): pl.pallas_call(functools.partial(project_kernel, devices), out_shape=(jax...  106 us
    pallas_call x1, Pallas kernels, attend(): pl.pallas_call(functools.partial(attend_kernel, devices), out_shape=jax.S...  50.4 us
    unnamed x5, local copies, waits for them, and re-layouts  10.2 us

profile of v3, /device:TPU:0, one launch (start us, length us, event | category | flops | bytes accessed | tf_op | source)
XLA Modules:
  0.0 170.4 jit_solution(6899897060033098073)
XLA Ops:
  0.6 1.4 reshape.17.gain_ref
  2.1 1.5 copy.14.parent_ref
  3.5 1.9 %copy.16 = bf16[256,8,128]{2,0,1:T(8,128)(2,1)} copy(bf16[256,8,128]{2,1,0:T(8,128)(2,1)} %param.10) | data formatting | bytes 1048576 | tf_op args[0]
  5.4 50.4 %shard_map.113.att_ref = bf16[256,1024]{1,0:T(8,128)(2,1)} custom-call(bf16[8,256,128]{2,1,0:T(8,128)(2,1)} %bitcast.7, bf16[8,16,128]{2,1,0:T(8,128)(2,1)} %node_key_ref.1, bf16[8,16,128]{2,1,0:T(8,128)(2,1)} %node_value_ref.1, bf16[8,256,128]{2,1,0:T(8,128)(2,1)} %cache_key_ref.1, bf16[8,256,128]{2,1,0:T(8,128)(2,1)} %cache_value_ref.1, ...), custom_call_target="tpu_custom_call" | custom-call | flops 4563402752 | bytes 2228224 | tf_op jit(solution)/shard_map/pallas_call | solution.py:598
  55.8 106.3 %shard_map.114 = (bf16[16,16,16384]{2,1,0:T(8,128)(2,1)}, bf16[16,16,128]{2,1,0:T(8,128)(2,1)}) custom-call(bf16[256,1024]{1,0:T(8,128)(2,1)} %shard_map.113.att_ref, bf16[1024,16384]{1,0:T(8,128)(2,1)} %weight_ref.1, bf16[16,16384]{1,0:T(8,128)(2,1)} %residual_ref.1, bf16[1,16384]{1,0:T(2,128)(2,1)} %reshape.17.gain_ref, ...), custom_call_target="tpu_custom_call" | custom-call | flops 8589934592 | bytes 33554432 | tf_op jit(solution)/shard_map/pallas_call | solution.py:352
  162.1 0.0 copy-start
  162.1 7.7 %copy.19 = bf16[256,16384]{1,0:T(8,128)(2,1)} copy(bf16[256,16384]{1,0:T(8,128)(2,1)} %bitcast.6) | data formatting | bytes 16777216
  169.8 0.0 copy-done
  169.8 0.6 copy.20
Async XLA Ops:
  162.1 7.7 %copy-start = (bf16[16,16,128]{2,1,0:T(8,128)(2,1)S(1)}, bf16[16,16,128]{2,1,0:T(8,128)(2,1)}, u32[]{:S(2)}) copy-start(bf16[16,16,128]{2,1,0:T(8,128)(2,1)} %get-tuple-element.5) | copy-start | bytes 196612

commit v4 on v3

--- a/solution.py
+++ b/solution.py
@@ -519,7 +519,7 @@
                 top[head] = jnp.broadcast_to(peak, (tok_count, size))
             return carry
 
-        lax.fori_loop(0, heads, body, 0, unroll=2)
+        lax.fori_loop(0, heads, body, 0, unroll=4)
 
     def collect(offset, which):
         for a in which:
@@ -561,17 +561,17 @@
         False,
     )
     collect(1, (0, 1))
+    collect(2, (0, 1))
+    collect(3, (0, 1))
     chunk(0, False)
 
     def advance(j, carry):
-        collect(2 * j, (0, 1))
-        collect(2 * j + 1, (0, 1))
+        collect(2 * j + 2, (0, 1))
+        collect(2 * j + 3, (0, 1))
         chunk(j, False)
         return carry
 
     lax.fori_loop(1, chips // 2 - 1, advance, 0)
-    collect(chips - 2, (0, 1))
-    collect(chips - 1, (0, 1))
     chunk(chips // 2 - 1, True)
 
     def drain(offset, carry):

time: 171 us -> 167 us (0.977)
  Pallas kernels: 157 us -> 153 us
    pallas_call x1, Pallas kernels: 50.4 us -> 42.1 us  [attend(): pl.pallas_call(functools.partial(attend_kernel, devices), out_shape=jax.S...]
    pallas_call x1, Pallas kernels: 106 us -> 111 us  [project(): pl.pallas_call(functools.partial(project_kernel, devices), out_shape=(jax...]
where the time goes in v4:
time: 167 us
  Pallas kernels  153 us (92%)
  local copies, waits for them, and re-layouts  13.1 us (8%)
    pallas_call x1, Pallas kernels, project(): pl.pallas_call(functools.partial(project_kernel, devices), out_shape=(jax...  111 us
    pallas_call x1, Pallas kernels, attend(): pl.pallas_call(functools.partial(attend_kernel, devices), out_shape=jax.S...  42.1 us
    unnamed x5, local copies, waits for them, and re-layouts  10.2 us

profile of v4, /device:TPU:0, one launch (start us, length us, event | category | flops | bytes accessed | tf_op | source)
XLA Modules:
  0.0 166.7 jit_solution(5031215121908280153)
XLA Ops:
  0.6 1.4 reshape.17.gain_ref
  2.1 1.5 copy.14.parent_ref
  3.5 1.9 %copy.16 = bf16[256,8,128]{2,0,1:T(8,128)(2,1)} copy(bf16[256,8,128]{2,1,0:T(8,128)(2,1)} %param.10) | data formatting | bytes 1048576 | tf_op args[0]
  5.4 42.1 %shard_map.113.att_ref = bf16[256,1024]{1,0:T(8,128)(2,1)} custom-call(bf16[8,256,128]{2,1,0:T(8,128)(2,1)} %bitcast.7, bf16[8,16,128]{2,1,0:T(8,128)(2,1)} %node_key_ref.1, bf16[8,16,128]{2,1,0:T(8,128)(2,1)} %node_value_ref.1, bf16[8,256,128]{2,1,0:T(8,128)(2,1)} %cache_key_ref.1, bf16[8,256,128]{2,1,0:T(8,128)(2,1)} %cache_value_ref.1, ...), custom_call_target="tpu_custom_call" | custom-call | flops 4563402752 | bytes 2228224 | tf_op jit(solution)/shard_map/pallas_call | solution.py:598
  47.5 110.8 %shard_map.114 = (bf16[16,16,16384]{2,1,0:T(8,128)(2,1)}, bf16[16,16,128]{2,1,0:T(8,128)(2,1)}) custom-call(bf16[256,1024]{1,0:T(8,128)(2,1)} %shard_map.113.att_ref, bf16[1024,16384]{1,0:T(8,128)(2,1)} %weight_ref.1, bf16[16,16384]{1,0:T(8,128)(2,1)} %residual_ref.1, bf16[1,16384]{1,0:T(2,128)(2,1)} %reshape.17.gain_ref, ...), custom_call_target="tpu_custom_call" | custom-call | flops 8589934592 | bytes 33554432 | tf_op jit(solution)/shard_map/pallas_call | solution.py:352
  158.4 0.0 copy-start
  158.4 7.7 %copy.19 = bf16[256,16384]{1,0:T(8,128)(2,1)} copy(bf16[256,16384]{1,0:T(8,128)(2,1)} %bitcast.6) | data formatting | bytes 16777216
  166.1 0.0 copy-done
  166.1 0.6 copy.20
Async XLA Ops:
  158.4 7.7 %copy-start = (bf16[16,16,128]{2,1,0:T(8,128)(2,1)S(1)}, bf16[16,16,128]{2,1,0:T(8,128)(2,1)}, u32[]{:S(2)}) copy-start(bf16[16,16,128]{2,1,0:T(8,128)(2,1)} %get-tuple-element.5) | copy-start | bytes 196612
